TPU v7x, 32 devices: a whole 2x2x4 slice. The times are simulated.
32 devices in a mesh: groups: 2 (over x), dp: 16 (over z, y, core).
Axes of the slice: x: 2, y: 2, z: 4, core: 2. Of those that a mesh axis runs over, the one named last changes fastest.
Arguments:
- train_acts: bfloat16 [8192, 8192], P(('groups', 'dp')), parts along dimension 0, may hold values from -6 to 6
- train_grads: bfloat16 [8192, 14336], P(('groups', 'dp')), parts along dimension 0
- lengths: int32 [64], P(('groups', 'dp')), parts along dimension 0, may hold values from 32 to 128
- query_in: bfloat16 [128, 8192], P('dp'), may hold values from -0.0625 to 0.0625
- query_out: bfloat16 [128, 14336], P('dp'), may hold values from -0.046875 to 0.046875
Outputs:
- influence: float32 [64, 4], P(('groups', 'dp')), parts along dimension 0
There are 2 independent parts, one for each index of `groups`. A program takes and returns all parts, laid end to end along the dimension named above; an argument that names none is the same for every part. Nothing has to cross between parts.
All inputs are finite; a program needn't handle non-finite values.
Results may differ from a plain program's by a relative error of at most 0.0003.
Values may be sent and summed in bfloat16 or wider, within the bound.
A program may use at most 128 MiB of HBM per device.

v0:
```python
import jax
import jax.numpy as jnp
from jax import lax
from jax.sharding import PartitionSpec as P

RANK = 32


def body(train_acts, train_grads, lengths, query_in, query_out):
    token_rows = train_acts.shape[0]
    seq_count = lengths.shape[0]
    seq_len = token_rows // seq_count
    device_count = lax.axis_size("dp")
    total_rows = query_in.shape[0] * device_count
    query_count = total_rows // RANK
    valid_mask = (jnp.arange(seq_len, dtype=jnp.int32)[None, :] < lengths[:, None]).astype(
        jnp.float32
    )
    all_left, all_right = (
        lax.all_gather(query_in, "dp", axis=0, tiled=True),
        lax.all_gather(query_out, "dp", axis=0, tiled=True),
    )
    left_proj = lax.dot_general(
        all_left, train_acts, (((1,), (1,)), ((), ())), preferred_element_type=jnp.float32
    )
    right_proj = lax.dot_general(
        all_right, train_grads, (((1,), (1,)), ((), ())), preferred_element_type=jnp.float32
    )
    product = (left_proj * right_proj).reshape(all_left.shape[0], seq_count, seq_len)
    onehot = (
        (jnp.arange(total_rows, dtype=jnp.int32) // RANK)[None, :]
        == jnp.arange(query_count, dtype=jnp.int32)[:, None]
    ).astype(jnp.float32)
    scores = jnp.dot(
        onehot, jnp.sum(product * valid_mask[None], axis=2), precision=lax.Precision.HIGHEST
    )
    squares = lax.psum(jnp.sum(scores * scores, axis=1), "dp")
    spread = squares / (seq_count * device_count)
    return (scores / jnp.sqrt(spread + 1e-06)[:, None]).T


def solution(mesh):
    in_specs = (
        P(("groups", "dp"), None),
        P(("groups", "dp"), None),
        P(("groups", "dp")),
        P("dp", None),
        P("dp", None),
    )
    out_specs = P(("groups", "dp"), None)
    return jax.shard_map(body, mesh=mesh, in_specs=in_specs, out_specs=out_specs, check_vma=False)
```

profile of v0, /device:TPU:0, one launch (start us, length us, event | category | flops | bytes accessed | tf_op | source)
XLA Modules:
  0.0 148.7 jit_solution(793377012308743342)
XLA Ops:
  6.5 0.0 all-gather.3.cloned.1.call-start
  6.5 0.7 all-gather.3.cloned.1.call-update
  7.3 0.0 all-gather.5.cloned.1.call-start
  7.3 0.7 all-gather.5.cloned.1.call-update
  8.0 0.7 compare_convert_fusion
  8.7 44.9 %all-gather.3.cloned.1.call-done = bf16[128,8192]{1,0:T(8,128)(2,1)} async-done(((bf16[8,8192]{1,0:T(8,128)(2,1)}), bf16[128,8192]{1,0:T(8,128)(2,1)}) %all-gather.3.cloned.1.call-update) | async-done | bytes 2097168 | tf_op jit(solution)/shard_map/all_gather | solution.py:20
  53.7 4.4 %fusion.2 = f32[128,256]{1,0:T(8,128)S(1)} fusion(bf16[128,8192]{1,0:T(8,128)(2,1)} %all-gather.3.cloned.1.call-done, bf16[256,8192]{1,0:T(8,128)(2,1)} %param.5), kind=kOutput, calls=%fused_computation.13 | convolution fusion | flops 536870912 | bytes 6422528 | tf_op jit(solution)/shard_map/dot_general | solution.py:23
  58.0 44.2 %all-gather.5.cloned.1.call-done = bf16[128,14336]{1,0:T(8,128)(2,1)} async-done(((bf16[8,14336]{1,0:T(8,128)(2,1)}), bf16[128,14336]{1,0:T(8,128)(2,1)}) %all-gather.5.cloned.1.call-update) | async-done | bytes 3670032 | tf_op jit(solution)/shard_map/all_gather | solution.py:21
  102.2 6.8 %convolution_multiply_fusion = f32[128,256]{1,0:T(8,128)S(1)} fusion(f32[128,256]{1,0:T(8,128)S(1)} %fusion.2, bf16[128,14336]{1,0:T(8,128)(2,1)} %all-gather.5.cloned.1.call-done, bf16[256,14336]{1,0:T(8,128)(2,1)} %param.6), kind=kOutput, calls=%fused_computation | convolution fusion | flops 939556864 | bytes 11272192 | tf_op jit(solution)/shard_map/dot_general | solution.py:26
  109.0 0.1 reshape.36
  109.1 0.2 multiply_reduce_fusion
  109.3 0.2 multiply_reduce_fusion.1
  109.5 31.7 %psum.7 = f32[4]{0:T(128)S(1)} all-reduce(f32[4]{0:T(128)S(1)} %get-tuple-element.5), channel_id=1, replica_groups=mesh['groups'=2,'dp'=16] {'dp'}, use_global_device_ids=true, to_apply=%region_2.3 | all-reduce | flops 4 | bytes 32 | tf_op jit(solution)/shard_map/psum | solution.py:37
  141.2 0.6 divide_bitcast_fusion
  (2 shorter events, 0.0 us)
Async XLA Ops:
  6.5 47.1 %all-gather.3.cloned.1.call-start = ((), (), s32[]{:S(2)}) async-start(), calls=%async_computation | async-start | bytes 2228224 | tf_op jit(solution)/shard_map/all_gather | solution.py:20
  7.3 95.0 %all-gather.5.cloned.1.call-start = ((), (), s32[]{:S(2)}) async-start(), calls=%async_computation.1 | async-start | bytes 3899392 | tf_op jit(solution)/shard_map/all_gather | solution.py:21
Sparse Core Ops, SparseCore 0:
  9.5 44.0 all-gather.2
  55.9 46.2 all-gather.4
where the time goes:
time: 149 us
  waiting for transfers between devices  90.5 us (61%)
  blocking collectives  31.7 us (21%)
  between operations  13.4 us (9%)
  matrix products  11.3 us (8%)
  other arithmetic  1.53 us (1%)
    all_gather x1, waiting for transfers between devices, body(): lax.all_gather(query_in, 'dp', axis=0, tiled=True)  44.9 us
    all_gather x1, waiting for transfers between devices, body(): lax.all_gather(query_out, 'dp', axis=0, tiled=True)  44.2 us
    psum x1, blocking collectives, body(): squares = lax.psum(jnp.sum(scores * scores, axis=1), 'dp')  31.7 us
    dot_general x1, matrix products, body(): lax.dot_general(all_right, train_grads, (((1,), (1,)), ((), ())), preferr...  6.78 us
    dot_general x1, matrix products, body(): lax.dot_general(all_left, train_acts, (((1,), (1,)), ((), ())), preferred...  4.35 us
  transfers between devices with their start and end apart: 2, of which 2 were waited for; matrix products, arithmetic and copies ran while one was open for 3% of the time, Pallas kernels for 0%

commit v1 on v0

--- a/solution.py
+++ b/solution.py
@@ -1,12 +1,18 @@
+import functools
+
 import jax
 import jax.numpy as jnp
 from jax import lax
+from jax.experimental import pallas as pl
+from jax.experimental.pallas import tpu as pltpu
 from jax.sharding import PartitionSpec as P
 
 RANK = 32
-
-
-def body(train_acts, train_grads, lengths, query_in, query_out):
+MESH = pl.DeviceIdType.MESH
+WIDTH = 2048
+
+
+def plain_body(train_acts, train_grads, lengths, query_in, query_out):
     token_rows = train_acts.shape[0]
     seq_count = lengths.shape[0]
     seq_len = token_rows // seq_count
@@ -39,6 +45,234 @@
     return (scores / jnp.sqrt(spread + 1e-06)[:, None]).T
 
 
+def make_plan(left_cols, right_cols):
+    chunks = {"l": left_cols // WIDTH, "r": right_cols // WIDTH}
+    total = chunks["l"] + chunks["r"]
+    both = max(1, round(total * 3 / 11))
+    if (total - both) % 2:
+        both += 1
+    plan = []
+    for k in range(chunks["l"] // 2):
+        plan.append(("pair", 0, 2 * k * WIDTH))
+    pairs_right = (chunks["r"] - both) // 2
+    for k in range(pairs_right):
+        plan.append(("pair", 1, 2 * k * WIDTH))
+    for k in range(2 * pairs_right, chunks["r"]):
+        plan.append(("both", 1, k * WIDTH))
+    return plan
+
+
+def count_copies(plan):
+    return sum(11 if kind == "pair" else 7 for kind, _, _ in plan)
+
+
+def kernel(
+    plan, seq_len, lengths_ref, acts_hbm, grads_hbm, qin_hbm, qout_hbm, out_ref,
+    acts, grads, left, right, acc_left, acc_right, squares, local_sem, send_sem, recv_sem,
+    sq_send, sq_recv,
+):
+    group = lax.axis_index("groups")
+    me = lax.axis_index("dp")
+    z, y, core = me // 4, (me // 2) % 2, me % 2
+
+    def at(dz=0, dy=0, dc=0):
+        return ((z + dz) % 4) * 4 + ((y + dy) % 2) * 2 + (core + dc) % 2
+
+    z_peers = [(group, at(dz=d)) for d in (1, 2, 3)]
+    y_peer = (group, at(dy=1))
+    core_peer = (group, at(dc=1))
+    x_peer = (1 - group, me)
+
+    own_left = pltpu.make_async_copy(qin_hbm, left.at[0, 0, 0], local_sem.at[0])
+    own_right = pltpu.make_async_copy(qout_hbm, right.at[0, 0, 0], local_sem.at[1])
+    load_acts = pltpu.make_async_copy(acts_hbm, acts, local_sem.at[2])
+    load_grads = pltpu.make_async_copy(grads_hbm, grads, local_sem.at[3])
+    own_left.start()
+    own_right.start()
+    load_acts.start()
+    load_grads.start()
+
+    barrier = pltpu.get_barrier_semaphore()
+    others = [(group, (me + d) % 16) for d in range(1, 16)]
+    for other in others + [x_peer]:
+        pl.semaphore_signal(barrier, inc=1, device_id=other, device_id_type=MESH)
+    pl.semaphore_wait(barrier, 16)
+    own_left.wait()
+    own_right.wait()
+
+    sides = (left, right)
+    acc_left[...] = jnp.zeros_like(acc_left)
+    acc_right[...] = jnp.zeros_like(acc_right)
+    next_id = [0]
+    sent = []
+
+    def send(src, dst, peer):
+        k = next_id[0]
+        next_id[0] += 1
+        copy = pltpu.make_async_remote_copy(
+            src_ref=src, dst_ref=dst, send_sem=send_sem.at[k], recv_sem=recv_sem.at[k],
+            device_id=peer, device_id_type=MESH,
+        )
+        return copy
+
+    steps = []
+    for kind, side, start in plan:
+        buf = sides[side]
+        step = dict(kind=kind, side=side, start=start)
+        if kind == "pair":
+            mine = pl.ds(pl.multiple_of(start + group * WIDTH, WIDTH), WIDTH)
+            theirs = pl.ds(pl.multiple_of(start + (1 - group) * WIDTH, WIDTH), WIDTH)
+        else:
+            mine = pl.ds(start, WIDTH)
+            theirs = None
+        step["z"] = [
+            send(buf.at[0, 0, 0, :, mine], buf.at[0, 0, 4 - d, :, mine], z_peers[d - 1])
+            for d in (1, 2, 3)
+        ]
+        step["y0"] = send(buf.at[0, 0, 0, :, mine], buf.at[0, 1, 0, :, mine], y_peer)
+        step["y"] = send(buf.at[0, 0, 1:4, :, mine], buf.at[0, 1, 1:4, :, mine], y_peer)
+        step["c0"] = send(buf.at[0, 0, :, :, mine], buf.at[1, 0, :, :, mine], core_peer)
+        step["c1"] = send(buf.at[0, 1, :, :, mine], buf.at[1, 1, :, :, mine], core_peer)
+        if kind == "pair":
+            step["x0"] = send(buf.at[0, 0, 1:4, :, mine], buf.at[0, 0, 1:4, :, mine], x_peer)
+            step["x1"] = send(buf.at[0, 1, :, :, mine], buf.at[0, 1, :, :, mine], x_peer)
+            step["x0r"] = buf.at[0, 0, 1:4, :, theirs]
+            step["x1r"] = buf.at[0, 1, :, :, theirs]
+            step["d0"] = send(buf.at[0, 0, :, :, theirs], buf.at[1, 0, :, :, theirs], core_peer)
+            step["d1"] = send(buf.at[0, 1, :, :, theirs], buf.at[1, 1, :, :, theirs], core_peer)
+        steps.append(step)
+
+    def go(copy):
+        copy.start()
+        sent.append(copy)
+
+    def bring(step):
+        for copy in step["z"]:
+            go(copy)
+        go(step["y0"])
+
+    def stage1(step):
+        for copy in step["z"]:
+            copy.wait_recv()
+        go(step["y"])
+        if step["kind"] == "pair":
+            go(step["x0"])
+        go(step["c0"])
+
+    def stage2(step):
+        step["y0"].wait_recv()
+        step["y"].wait_recv()
+        if step["kind"] == "pair":
+            go(step["x1"])
+        go(step["c1"])
+
+    def stage3(step):
+        if step["kind"] == "pair":
+            step["x0"].wait_recv()
+            go(step["d0"])
+            step["x1"].wait_recv()
+            go(step["d1"])
+
+    loaded = [False, False]
+
+    def stage4(step):
+        step["c0"].wait_recv()
+        step["c1"].wait_recv()
+        if step["kind"] == "pair":
+            step["d0"].wait_recv()
+            step["d1"].wait_recv()
+        side, start = step["side"], step["start"]
+        if not loaded[side]:
+            (load_acts, load_grads)[side].wait()
+            loaded[side] = True
+        width = WIDTH * (2 if step["kind"] == "pair" else 1)
+        rows = sides[side][:, :, :, :, start:start + width].reshape(128, width)
+        tokens = (acts, grads)[side][:, start:start + width]
+        acc = (acc_left, acc_right)[side]
+        acc[...] += lax.dot_general(
+            rows, tokens, (((1,), (1,)), ((), ())), preferred_element_type=jnp.float32
+        )
+
+    for step in steps:
+        bring(step)
+    stages = (stage1, stage2, stage3, stage4)
+    for i in range(len(steps) + 3):
+        for lag, stage in enumerate(stages):
+            if 0 <= i - lag < len(steps):
+                stage(steps[i - lag])
+
+    product = acc_left[...] * acc_right[...]
+    tokens = product.shape[1]
+    product = product.reshape(4, 4, 8, tokens)
+    by_query = product[0] + product[1] + product[2] + product[3]
+    row = lax.broadcasted_iota(jnp.int32, (8, 128), 0)
+    lane = lax.broadcasted_iota(jnp.int32, (8, 128), 1)
+    scores = jnp.zeros((8, 128), jnp.float32)
+    for n in range(2):
+        valid = lax.broadcasted_iota(jnp.int32, (8, seq_len), 1) < lengths_ref[n]
+        for d in range(4):
+            part = jnp.where(valid, by_query[d, :, n * seq_len:(n + 1) * seq_len], 0.0)
+            total = jnp.sum(jnp.sum(part, axis=0, keepdims=True), axis=1, keepdims=True)
+            scores += jnp.where((row == n) & (lane == (z + d) % 4), total, 0.0)
+
+    squares[0] = scores * scores
+    spreads = []
+    for d in range(1, 16):
+        copy = pltpu.make_async_remote_copy(
+            src_ref=squares.at[0], dst_ref=squares.at[d], send_sem=sq_send.at[d - 1],
+            recv_sem=sq_recv.at[d - 1], device_id=others[d - 1], device_id_type=MESH,
+        )
+        copy.start()
+        spreads.append(copy)
+    for copy in sent:
+        copy.wait_send()
+    for copy in spreads:
+        copy.wait_recv()
+    total = jnp.sum(jnp.sum(squares[...], axis=0), axis=0, keepdims=True)
+    spread = total / 32.0
+    out_ref[...] = scores / jnp.sqrt(spread + 1e-06)
+    for copy in spreads:
+        copy.wait_send()
+
+
+def kernel_body(train_acts, train_grads, lengths, query_in, query_out):
+    tokens, left_cols = train_acts.shape
+    right_cols = train_grads.shape[1]
+    seq_len = tokens // lengths.shape[0]
+    plan = make_plan(left_cols, right_cols)
+    copies = count_copies(plan)
+    anywhere = pl.BlockSpec(memory_space=pl.ANY)
+    tile = pl.pallas_call(
+        functools.partial(kernel, plan, seq_len),
+        out_shape=jax.ShapeDtypeStruct((8, 128), jnp.float32),
+        in_specs=[pl.BlockSpec(memory_space=pltpu.SMEM)] + [anywhere] * 4,
+        out_specs=pl.BlockSpec(memory_space=pltpu.VMEM),
+        scratch_shapes=[
+            pltpu.VMEM((tokens, left_cols), jnp.bfloat16),
+            pltpu.VMEM((tokens, right_cols), jnp.bfloat16),
+            pltpu.VMEM((2, 2, 4, 8, left_cols), jnp.bfloat16),
+            pltpu.VMEM((2, 2, 4, 8, right_cols), jnp.bfloat16),
+            pltpu.VMEM((128, tokens), jnp.float32),
+            pltpu.VMEM((128, tokens), jnp.float32),
+            pltpu.VMEM((16, 8, 128), jnp.float32),
+            pltpu.SemaphoreType.DMA((4,)),
+            pltpu.SemaphoreType.DMA((copies,)),
+            pltpu.SemaphoreType.DMA((copies,)),
+            pltpu.SemaphoreType.DMA((15,)),
+            pltpu.SemaphoreType.DMA((15,)),
+        ],
+        compiler_params=pltpu.CompilerParams(
+            collective_id=0, has_side_effects=True, vmem_limit_bytes=56 * 2**20
+        ),
+        cost_estimate=pl.CostEstimate(
+            flops=2 * 128 * tokens * (left_cols + right_cols),
+            bytes_accessed=2 * tokens * (left_cols + right_cols),
+            transcendentals=0,
+        ),
+    )(lengths, train_acts, train_grads, query_in, query_out)
+    return tile[:2, :4]
+
+
 def solution(mesh):
     in_specs = (
         P(("groups", "dp"), None),
@@ -48,4 +282,8 @@
         P("dp", None),
     )
     out_specs = P(("groups", "dp"), None)
-    return jax.shard_map(body, mesh=mesh, in_specs=in_specs, out_specs=out_specs, check_vma=False)
+    here = mesh.shape["groups"] == 2 and mesh.shape["dp"] == 16
+    return jax.shard_map(
+        kernel_body if here else plain_body,
+        mesh=mesh, in_specs=in_specs, out_specs=out_specs, check_vma=False,
+    )

time: 149 us -> 50.3 us (0.34)
  waiting for transfers between devices: 90.5 us -> 0 us
  Pallas kernels: 0 us -> 48.8 us
  blocking collectives: 31.7 us -> 0 us
  between operations: 13.4 us -> 0.01 us
  matrix products: 11.3 us -> 0 us
  other arithmetic: 1.53 us -> 0 us
    all_gather x2 -> x0, waiting for transfers between devices: 89.1 us -> none  [the longest x1 44.9 us: body(): lax.all_gather(query_in, 'dp', axis=0, tiled=True)]
    pallas_call x0 -> x1, Pallas kernels: none -> 48.8 us  [kernel_body(): pl.pallas_call(functools.partial(kernel, plan, seq_len), out_shape=jax.Sh...]
    psum x1 -> x0, blocking collectives: 31.7 us -> none  [body(): squares = lax.psum(jnp.sum(scores * scores, axis=1), 'dp')]
    dot_general x3 -> x0, matrix products: 11.3 us -> none  [the longest x1 6.78 us: body(): lax.dot_general(all_right, train_grads, (((1,), (1,)), ((), ())), preferr...]
  transfers between devices with their start and end apart: 2 -> 0, of which waited for: 2 -> 0; matrix products, arithmetic and copies ran while one was open for 3% -> 0% of each run, Pallas kernels for 0% -> 0%
where the time goes in v1:
time: 50.3 us; the launch traced here: 50.1 us
  Pallas kernels  48.8 us (97%)
  local copies, waits for them, and re-layouts  1.25 us (2%)
    pallas_call x1, Pallas kernels, kernel_body(): pl.pallas_call(functools.partial(kernel, plan, seq_len), out_shape=jax.Sh...  48.8 us
    slice x1, local copies, waits for them, and re-layouts, kernel_body(): return tile[:2, :4]  1.25 us

profile of v1, /device:TPU:0, one launch (start us, length us, event | category | flops | bytes accessed | tf_op | source)
XLA Modules:
  0.0 50.1 jit_solution(18119945598897332227)
XLA Ops:
  0.0 48.8 %shard_map.55 = f32[8,128]{1,0:T(8,128)} custom-call(s32[2]{0:T(128)} %lengths_ref.1, bf16[256,8192]{1,0:T(8,128)(2,1)} %acts_hbm.1, bf16[256,14336]{1,0:T(8,128)(2,1)} %grads_hbm.1, bf16[8,8192]{1,0:T(8,128)(2,1)} %qin_hbm.1, bf16[8,14336]{1,0:T(8,128)(2,1)} %qout_hbm.1), custom_call_target="tpu_custom_call" | custom-call | flops 1476395008 | bytes 11534336 | tf_op jit(solution)/shard_map/pallas_call | solution.py:245
  48.8 1.2 %slice.3 = f32[2,4]{1,0:T(2,128)} slice(f32[8,128]{1,0:T(8,128)} %shard_map.55), slice={[0:2], [0:4]} | slice | bytes 64 | tf_op jit(solution)/shard_map/slice | solution.py:273

commit v2 on v1

--- a/solution.py
+++ b/solution.py
@@ -10,6 +10,8 @@
 RANK = 32
 MESH = pl.DeviceIdType.MESH
 WIDTH = 2048
+AHEAD = 2
+LATENCY = 3.0
 
 
 def plain_body(train_acts, train_grads, lengths, query_in, query_out):
@@ -60,6 +62,28 @@
     for k in range(2 * pairs_right, chunks["r"]):
         plan.append(("both", 1, k * WIDTH))
     return plan
+
+
+def make_order(plan):
+    events, asks = [], []
+    z_free = y_free = x_free = 0.0
+    ready = []
+    for i, (kind, _, _) in enumerate(plan):
+        z_free += 4.0
+        z_in = z_free + LATENCY
+        y_free = max(y_free, z_in) + (3.0 if i < AHEAD else 4.0)
+        y_in = y_free + LATENCY
+        events += [(z_in, i, "z"), (y_in, i, "y")]
+        ready.append(y_in)
+        if kind == "pair":
+            asks += [(z_in, i, "x0", 3.0), (y_in, i, "x1", 4.0)]
+    for time, i, name, blocks in sorted(asks):
+        x_free = max(x_free, time) + blocks
+        events.append((x_free + LATENCY, i, name))
+        ready[i] = max(ready[i], x_free + LATENCY)
+    for i, time in enumerate(ready):
+        events.append((time + LATENCY, i, "done"))
+    return sorted(events)
 
 
 def count_copies(plan):
@@ -166,12 +190,13 @@
             go(step["x1"])
         go(step["c1"])
 
-    def stage3(step):
-        if step["kind"] == "pair":
-            step["x0"].wait_recv()
-            go(step["d0"])
-            step["x1"].wait_recv()
-            go(step["d1"])
+    def stage3a(step):
+        step["x0"].wait_recv()
+        go(step["d0"])
+
+    def stage3b(step):
+        step["x1"].wait_recv()
+        go(step["d1"])
 
     loaded = [False, False]
 
@@ -193,13 +218,15 @@
             rows, tokens, (((1,), (1,)), ((), ())), preferred_element_type=jnp.float32
         )
 
-    for step in steps:
+    for step in steps[:AHEAD]:
         bring(step)
-    stages = (stage1, stage2, stage3, stage4)
-    for i in range(len(steps) + 3):
-        for lag, stage in enumerate(stages):
-            if 0 <= i - lag < len(steps):
-                stage(steps[i - lag])
+    brought = AHEAD
+    stages = dict(z=stage1, y=stage2, x0=stage3a, x1=stage3b, done=stage4)
+    for _, i, name in make_order(plan):
+        stages[name](steps[i])
+        if name == "z" and brought < len(steps):
+            bring(steps[brought])
+            brought += 1
 
     product = acc_left[...] * acc_right[...]
     tokens = product.shape[1]

time: 50.3 us -> 44.8 us (0.89)
  Pallas kernels: 48.8 us -> 43.4 us
    pallas_call x1, Pallas kernels: 48.8 us -> 43.4 us  [kernel_body(): pl.pallas_call(functools.partial(kernel, plan, seq_len), out_shape=jax.Sh...]
where the time goes in v2:
time: 44.8 us; the launch traced here: 44.6 us
  Pallas kernels  43.4 us (97%)
  local copies, waits for them, and re-layouts  1.25 us (3%)
    pallas_call x1, Pallas kernels, kernel_body(): pl.pallas_call(functools.partial(kernel, plan, seq_len), out_shape=jax.Sh...  43.4 us
    slice x1, local copies, waits for them, and re-layouts, kernel_body(): return tile[:2, :4]  1.25 us

profile of v2, /device:TPU:0, one launch (start us, length us, event | category | flops | bytes accessed | tf_op | source)
XLA Modules:
  0.0 44.6 jit_solution(10598426004249157004)
XLA Ops:
  0.0 43.4 %shard_map.55 = f32[8,128]{1,0:T(8,128)} custom-call(s32[2]{0:T(128)} %lengths_ref.1, bf16[256,8192]{1,0:T(8,128)(2,1)} %acts_hbm.1, bf16[256,14336]{1,0:T(8,128)(2,1)} %grads_hbm.1, bf16[8,8192]{1,0:T(8,128)(2,1)} %qin_hbm.1, bf16[8,14336]{1,0:T(8,128)(2,1)} %qout_hbm.1), custom_call_target="tpu_custom_call" | custom-call | flops 1476395008 | bytes 11534336 | tf_op jit(solution)/shard_map/pallas_call | solution.py:272
  43.4 1.2 %slice.3 = f32[2,4]{1,0:T(2,128)} slice(f32[8,128]{1,0:T(8,128)} %shard_map.55), slice={[0:2], [0:4]} | slice | bytes 64 | tf_op jit(solution)/shard_map/slice | solution.py:300

commit v3 on v2

--- a/solution.py
+++ b/solution.py
@@ -9,7 +9,9 @@
 
 RANK = 32
 MESH = pl.DeviceIdType.MESH
-WIDTH = 2048
+LEFT_PAIRS = (2048, 2048)
+RIGHT_PAIRS = (2048, 1024)
+BOTH = (2048, 2048, 2048, 2048)
 AHEAD = 2
 LATENCY = 3.0
 
@@ -48,19 +50,20 @@
 
 
 def make_plan(left_cols, right_cols):
-    chunks = {"l": left_cols // WIDTH, "r": right_cols // WIDTH}
-    total = chunks["l"] + chunks["r"]
-    both = max(1, round(total * 3 / 11))
-    if (total - both) % 2:
-        both += 1
     plan = []
-    for k in range(chunks["l"] // 2):
-        plan.append(("pair", 0, 2 * k * WIDTH))
-    pairs_right = (chunks["r"] - both) // 2
-    for k in range(pairs_right):
-        plan.append(("pair", 1, 2 * k * WIDTH))
-    for k in range(2 * pairs_right, chunks["r"]):
-        plan.append(("both", 1, k * WIDTH))
+
+    def add(kind, side, start, count, widths):
+        for k in range(len(widths)):
+            width = widths[k]
+            plan.append((kind, side, start, width))
+            start += width * (2 if kind == "pair" else 1)
+            count -= width * (2 if kind == "pair" else 1)
+        assert count == 0
+        return start
+
+    add("pair", 0, 0, left_cols, LEFT_PAIRS)
+    start = add("pair", 1, 0, 2 * sum(RIGHT_PAIRS), RIGHT_PAIRS)
+    add("both", 1, start, right_cols - start, BOTH)
     return plan
 
 
@@ -68,15 +71,16 @@
     events, asks = [], []
     z_free = y_free = x_free = 0.0
     ready = []
-    for i, (kind, _, _) in enumerate(plan):
-        z_free += 4.0
+    for i, (kind, _, _, width) in enumerate(plan):
+        block = width / 2048
+        z_free += 4.0 * block
         z_in = z_free + LATENCY
-        y_free = max(y_free, z_in) + (3.0 if i < AHEAD else 4.0)
+        y_free = max(y_free, z_in) + 3.0 * block
         y_in = y_free + LATENCY
         events += [(z_in, i, "z"), (y_in, i, "y")]
         ready.append(y_in)
         if kind == "pair":
-            asks += [(z_in, i, "x0", 3.0), (y_in, i, "x1", 4.0)]
+            asks += [(z_in, i, "x0", 3.0 * block), (y_in, i, "x1", 4.0 * block)]
     for time, i, name, blocks in sorted(asks):
         x_free = max(x_free, time) + blocks
         events.append((x_free + LATENCY, i, name))
@@ -87,7 +91,7 @@
 
 
 def count_copies(plan):
-    return sum(11 if kind == "pair" else 7 for kind, _, _ in plan)
+    return sum(11 if step[0] == "pair" else 7 for step in plan)
 
 
 def kernel(
@@ -140,14 +144,14 @@
         return copy
 
     steps = []
-    for kind, side, start in plan:
+    for kind, side, start, width in plan:
         buf = sides[side]
-        step = dict(kind=kind, side=side, start=start)
+        step = dict(kind=kind, side=side, start=start, width=width)
         if kind == "pair":
-            mine = pl.ds(pl.multiple_of(start + group * WIDTH, WIDTH), WIDTH)
-            theirs = pl.ds(pl.multiple_of(start + (1 - group) * WIDTH, WIDTH), WIDTH)
+            mine = pl.ds(pl.multiple_of(start + group * width, 128), width)
+            theirs = pl.ds(pl.multiple_of(start + (1 - group) * width, 128), width)
         else:
-            mine = pl.ds(start, WIDTH)
+            mine = pl.ds(start, width)
             theirs = None
         step["z"] = [
             send(buf.at[0, 0, 0, :, mine], buf.at[0, 0, 4 - d, :, mine], z_peers[d - 1])
@@ -173,7 +177,6 @@
     def bring(step):
         for copy in step["z"]:
             go(copy)
-        go(step["y0"])
 
     def stage1(step):
         for copy in step["z"]:
@@ -199,6 +202,7 @@
         go(step["d1"])
 
     loaded = [False, False]
+    pieces = []
 
     def stage4(step):
         step["c0"].wait_recv()
@@ -210,7 +214,12 @@
         if not loaded[side]:
             (load_acts, load_grads)[side].wait()
             loaded[side] = True
-        width = WIDTH * (2 if step["kind"] == "pair" else 1)
+        width = step["width"] * (2 if step["kind"] == "pair" else 1)
+        for piece in range(start, start + width, 2048):
+            pieces.append((side, piece, 2048))
+
+    def multiply():
+        side, start, width = pieces.pop(0)
         rows = sides[side][:, :, :, :, start:start + width].reshape(128, width)
         tokens = (acts, grads)[side][:, start:start + width]
         acc = (acc_left, acc_right)[side]
@@ -220,6 +229,8 @@
 
     for step in steps[:AHEAD]:
         bring(step)
+    for step in steps:
+        go(step["y0"])
     brought = AHEAD
     stages = dict(z=stage1, y=stage2, x0=stage3a, x1=stage3b, done=stage4)
     for _, i, name in make_order(plan):
@@ -227,6 +238,10 @@
         if name == "z" and brought < len(steps):
             bring(steps[brought])
             brought += 1
+        if pieces:
+            multiply()
+    while pieces:
+        multiply()
 
     product = acc_left[...] * acc_right[...]
     tokens = product.shape[1]

time: 44.8 us -> 44 us (0.982)
  Pallas kernels: 43.4 us -> 42.5 us
    pallas_call x1, Pallas kernels: 43.4 us -> 42.5 us  [kernel_body(): pl.pallas_call(functools.partial(kernel, plan, seq_len), out_shape=jax.Sh...]
where the time goes in v3:
time: 44 us; the launch traced here: 43.8 us
  Pallas kernels  42.5 us (97%)
  local copies, waits for them, and re-layouts  1.25 us (3%)
    pallas_call x1, Pallas kernels, kernel_body(): pl.pallas_call(functools.partial(kernel, plan, seq_len), out_shape=jax.Sh...  42.5 us
    slice x1, local copies, waits for them, and re-layouts, kernel_body(): return tile[:2, :4]  1.25 us

profile of v3, /device:TPU:0, one launch (start us, length us, event | category | flops | bytes accessed | tf_op | source)
XLA Modules:
  0.0 43.8 jit_solution(3759769660892455432)
XLA Ops:
  0.0 42.5 %shard_map.55 = f32[8,128]{1,0:T(8,128)} custom-call(s32[2]{0:T(128)} %lengths_ref.1, bf16[256,8192]{1,0:T(8,128)(2,1)} %acts_hbm.1, bf16[256,14336]{1,0:T(8,128)(2,1)} %grads_hbm.1, bf16[8,8192]{1,0:T(8,128)(2,1)} %qin_hbm.1, bf16[8,14336]{1,0:T(8,128)(2,1)} %qout_hbm.1), custom_call_target="tpu_custom_call" | custom-call | flops 1476395008 | bytes 11534336 | tf_op jit(solution)/shard_map/pallas_call | solution.py:287
  42.5 1.2 %slice.3 = f32[2,4]{1,0:T(2,128)} slice(f32[8,128]{1,0:T(8,128)} %shard_map.55), slice={[0:2], [0:4]} | slice | bytes 64 | tf_op jit(solution)/shard_map/slice | solution.py:315

commit v4 on v3

--- a/solution.py
+++ b/solution.py
@@ -11,7 +11,7 @@
 MESH = pl.DeviceIdType.MESH
 LEFT_PAIRS = (2048, 2048)
 RIGHT_PAIRS = (2048, 1024)
-BOTH = (2048, 2048, 2048, 2048)
+BOTH = (2048, 2048, 2048, 1024, 1024)
 AHEAD = 2
 LATENCY = 3.0
 
@@ -216,7 +216,7 @@
             loaded[side] = True
         width = step["width"] * (2 if step["kind"] == "pair" else 1)
         for piece in range(start, start + width, 2048):
-            pieces.append((side, piece, 2048))
+            pieces.append((side, piece, min(2048, width)))
 
     def multiply():
         side, start, width = pieces.pop(0)

time: 44 us -> 44.7 us (1.016)
  Pallas kernels: 42.5 us -> 43.2 us
    pallas_call x1, Pallas kernels: 42.5 us -> 43.2 us  [kernel_body(): pl.pallas_call(functools.partial(kernel, plan, seq_len), out_shape=jax.Sh...]
where the time goes in v4:
time: 44.7 us; the launch traced here: 44.5 us
  Pallas kernels  43.2 us (97%)
  local copies, waits for them, and re-layouts  1.25 us (3%)
    pallas_call x1, Pallas kernels, kernel_body(): pl.pallas_call(functools.partial(kernel, plan, seq_len), out_shape=jax.Sh...  43.2 us
    slice x1, local copies, waits for them, and re-layouts, kernel_body(): return tile[:2, :4]  1.25 us

profile of v4, /device:TPU:0, one launch (start us, length us, event | category | flops | bytes accessed | tf_op | source)
XLA Modules:
  0.0 44.5 jit_solution(6829566724463372669)
XLA Ops:
  0.0 43.2 %shard_map.55 = f32[8,128]{1,0:T(8,128)} custom-call(s32[2]{0:T(128)} %lengths_ref.1, bf16[256,8192]{1,0:T(8,128)(2,1)} %acts_hbm.1, bf16[256,14336]{1,0:T(8,128)(2,1)} %grads_hbm.1, bf16[8,8192]{1,0:T(8,128)(2,1)} %qin_hbm.1, bf16[8,14336]{1,0:T(8,128)(2,1)} %qout_hbm.1), custom_call_target="tpu_custom_call" | custom-call | flops 1476395008 | bytes 11534336 | tf_op jit(solution)/shard_map/pallas_call | solution.py:287
  43.2 1.2 %slice.3 = f32[2,4]{1,0:T(2,128)} slice(f32[8,128]{1,0:T(8,128)} %shard_map.55), slice={[0:2], [0:4]} | slice | bytes 64 | tf_op jit(solution)/shard_map/slice | solution.py:315
